TPU v7x, 32 devices: a whole 2x2x4 slice. The times are simulated.
32 devices in a mesh: groups: 2 (over y), slab: 4 (over z), pair: 4 (over x, core).
Axes of the slice: x: 2, y: 2, z: 4, core: 2. Of those that a mesh axis runs over, the one named last changes fastest.
Arguments:
- occupancy: float32 [8, 128, 256, 128], P(('groups', 'pair'), 'slab'), parts along dimension 0, may hold values from 0 to 1
- classes: int32 [8, 128, 256, 128], P(('groups', 'pair'), 'slab'), parts along dimension 0, may hold values from 0 to 7
- conductance: float32 [8], replicated, may hold values from 0.1 to 1
- damping: float32 [8], P('groups'), parts along dimension 0, may hold values from 1 to 8
- matches: int32 [8], P('groups'), parts along dimension 0, may hold values from 0 to 3, each once
Outputs:
- correlation: float32 [8, 128, 256, 128], P(('groups', 'pair'), 'slab'), parts along dimension 0
There are 2 independent parts, one for each index of `groups`. A program takes and returns all parts, laid end to end along the dimension named above; an argument that names none is the same for every part. Nothing has to cross between parts.
Inputs may be any that keep to these rules, and one draw needn't show every extreme that they name: A permutation of the 4 submaps; submap s is registered against submap matches[s]. `classes`: a row of the conductance table.
All inputs are finite; a program needn't handle non-finite values.
Results may differ from a plain program's by a relative error of at most 0.0003.
Values sent between devices are 32-bit elements; how exact they have to be, the bound alone decides.
A program may use at most 128 MiB of HBM per device.

v0:
```python
import math

import jax
import jax.numpy as jnp
from jax import lax
from jax.sharding import PartitionSpec as P

X = 256
STEPS = 4


STEP_SIZE = 1.0 / 6.0
FLOOR_VALUE = 0.01
FORMS = {1: "bjxy,jk->bkxy", 2: "bzjy,jk->bzky", 3: "bzxj,jk->bzxk"}


def with_halo(shard, sides, width):
    for axis, dim in sides:
        size, length = (lax.axis_size(axis), shard.shape[dim])
        up = [(i, (i + 1) % size) for i in range(size - 1)]
        down = [(j, i) for i, j in up]
        last = lax.slice_in_dim(shard, length - width, length, axis=dim)
        leading = lax.slice_in_dim(shard, 0, width, axis=dim)
        before = lax.ppermute(last, axis, up)
        after = lax.ppermute(leading, axis, down)
        shard = jnp.concatenate([before, shard, after], axis=dim)
    return shard


def tables(length):
    counter = jnp.arange(length, dtype=jnp.int32)
    product = counter[:, None] * counter[None, :] % length
    angles = product.astype(jnp.float32) * (2.0 * math.pi / length)
    factor = 1.0 / math.sqrt(length)
    return (jnp.cos(angles) * factor, jnp.sin(angles) * factor)


def multiply_along(values, matrix, axis_dim):
    return jnp.einsum(FORMS[axis_dim], values, matrix, precision=lax.Precision.HIGHEST)


def forward_real(values, axis_dim):
    cosine, sine_table = tables(values.shape[axis_dim])
    return (multiply_along(values, cosine, axis_dim), -multiply_along(values, sine_table, axis_dim))


def forward_complex(real_part, imag_part, axis_dim):
    cosine, sine_table = tables(real_part.shape[axis_dim])
    return (
        multiply_along(real_part, cosine, axis_dim)
        + multiply_along(imag_part, sine_table, axis_dim),
        multiply_along(imag_part, cosine, axis_dim)
        - multiply_along(real_part, sine_table, axis_dim),
    )


def inverse_complex(real_part, imag_part, axis_dim):
    cosine, sine_table = tables(real_part.shape[axis_dim])
    return (
        multiply_along(real_part, cosine, axis_dim)
        - multiply_along(imag_part, sine_table, axis_dim),
        multiply_along(imag_part, cosine, axis_dim)
        + multiply_along(real_part, sine_table, axis_dim),
    )


def inverse_real(real_part, imag_part, axis_dim):
    cosine, sine_table = tables(real_part.shape[axis_dim])
    return multiply_along(real_part, cosine, axis_dim) - multiply_along(
        imag_part, sine_table, axis_dim
    )


def local_neighbours(padded):
    widened = jnp.pad(padded, ((0, 0), (0, 0), (1, 1), (1, 1)))
    return [
        widened[:, 2:, 1:-1, 1:-1],
        widened[:, :-2, 1:-1, 1:-1],
        widened[:, 1:-1, 2:, 1:-1],
        widened[:, 1:-1, :-2, 1:-1],
        widened[:, 1:-1, 1:-1, 2:],
        widened[:, 1:-1, 1:-1, :-2],
    ]


def signed_frequency(counter, length):
    return jnp.where(counter < length // 2, counter, counter - length).astype(jnp.float32) / length


def cross_power(own_real, own_imag, far_real, far_imag, decay_rate, offset):
    depth_count = own_real.shape[1]
    row_count = own_real.shape[2]
    width_count = own_real.shape[3]
    along_depth = signed_frequency(jnp.arange(depth_count, dtype=jnp.int32), depth_count)
    along_rows = signed_frequency(offset + jnp.arange(row_count, dtype=jnp.int32), X)
    along_width = signed_frequency(jnp.arange(width_count, dtype=jnp.int32), width_count)
    radius = (
        along_depth[:, None, None] ** 2
        + along_rows[None, :, None] ** 2
        + along_width[None, None, :] ** 2
    )
    cross_real = own_real * far_real + own_imag * far_imag
    cross_imag = own_imag * far_real - own_real * far_imag
    magnitude = jnp.sqrt((own_real**2 + own_imag**2) * (far_real**2 + far_imag**2) + FLOOR_VALUE**2)
    weight = jnp.exp(-decay_rate[:, None, None, None] * radius[None]) / magnitude
    return (cross_real * weight, cross_imag * weight)


def local(occupancy, classes, conductance, damping, matches):
    conduct = jnp.zeros(occupancy.shape, jnp.float32)
    for class_id in range(conductance.shape[0]):
        conduct = jnp.where(classes == class_id, conductance[class_id], conduct)
    outer_rims = local_neighbours(with_halo(conduct, (("slab", 1),), 1))
    volume = occupancy
    for sweep_index in range(STEPS):
        beside_all = local_neighbours(with_halo(volume, (("slab", 1),), 1))
        change = jnp.zeros_like(volume)
        for other_field, other_conduct in zip(beside_all, outer_rims):
            change = change + 0.5 * (conduct + other_conduct) * (other_field - volume)
        volume = volume + STEP_SIZE * change
    real_part, imag_part = forward_real(volume, 3)
    real_part, imag_part = forward_complex(real_part, imag_part, 2)
    real_part, imag_part = (
        lax.all_to_all(
            lax.all_to_all(real_part, "pair", split_axis=2, concat_axis=0, tiled=True),
            "slab",
            split_axis=2,
            concat_axis=1,
            tiled=True,
        ),
        lax.all_to_all(
            lax.all_to_all(imag_part, "pair", split_axis=2, concat_axis=0, tiled=True),
            "slab",
            split_axis=2,
            concat_axis=1,
            tiled=True,
        ),
    )
    real_part, imag_part = forward_complex(real_part, imag_part, 1)
    far_real = jnp.take(real_part, matches, axis=0)
    far_imag = jnp.take(imag_part, matches, axis=0)
    offset = (
        lax.axis_index("pair") * lax.axis_size("slab") + lax.axis_index("slab")
    ) * real_part.shape[2]
    cross_real, cross_imag = cross_power(real_part, imag_part, far_real, far_imag, damping, offset)
    cross_real, cross_imag = inverse_complex(cross_real, cross_imag, 1)
    back_real, back_imag = (
        lax.all_to_all(
            lax.all_to_all(cross_real, "slab", split_axis=1, concat_axis=2, tiled=True),
            "pair",
            split_axis=0,
            concat_axis=2,
            tiled=True,
        ),
        lax.all_to_all(
            lax.all_to_all(cross_imag, "slab", split_axis=1, concat_axis=2, tiled=True),
            "pair",
            split_axis=0,
            concat_axis=2,
            tiled=True,
        ),
    )
    back_real, back_imag = inverse_complex(back_real, back_imag, 2)
    return inverse_real(back_real, back_imag, 3)


def solution(mesh):
    in_specs = (
        P(("groups", "pair"), "slab", None, None),
        P(("groups", "pair"), "slab", None, None),
        P(),
        P("groups"),
        P("groups"),
    )
    out_specs = P(("groups", "pair"), "slab", None, None)
    return jax.shard_map(local, mesh=mesh, in_specs=in_specs, out_specs=out_specs, check_vma=False)
```

profile of v0, /device:TPU:9, one launch (start us, length us, event | category | flops | bytes accessed | tf_op | source)
XLA Modules:
  0.0 885.0 jit_solution(9573891897190911826)
XLA Ops:
  1.6 9.0 %select_select_fusion = f32[1,32,256,128]{3,2,1,0:T(8,128)S(1)} fusion(s32[1,32,256,128]{3,2,1,0:T(8,128)} %param.8, f32[]{:T(128)} %bitcast.10, f32[]{:T(128)} %bitcast.9, f32[]{:T(128)} %bitcast.8, f32[]{:T(128)} %bitcast.7, f32[]{:T(128)} %bitcast.6, f32[]{:T(128)} %bitcast.5, f32[]{:T(128)} %bitcast.4, f32[]{:T(128)} %bitcast.3), kind=kLoop, calls=%fused_computation.138 | loop fusion | flops 16777216 | bytes 8388640 | tf_op jit(solution)/shard_map/jit(_where)/select_n | solution.py:112
  12.6 3.4 collective-permute-start.2
  17.9 3.4 collective-permute-start.3
  21.3 4.4 select_maximum_fusion.8
  25.7 6.3 select_maximum_fusion.6
  32.1 25.3 %fusion.52 = f32[1,32,256,128]{3,2,1,0:T(8,128)} fusion(f32[1,32,256,128]{3,2,1,0:T(8,128)} %param.7, f32[1,34,258,130]{3,2,1,0:T(8,128)} %select_maximum_fusion.6, f32[1,1,256,128]{3,2,1,0:T(8,128)S(1)} %collective-permute-done.3, f32[1,1,256,128]{3,2,1,0:T(8,128)S(1)} %collective-permute-done.1, f32[1,32,256,128]{3,2,1,0:T(8,128)} %copy-done, ...), kind=kLoop, calls=%fused_computation.87 | loop fusion | flops 36700160 | bytes 46661632 | tf_op jit(solution)/shard_map/add | solution.py:120
  60.3 3.4 collective-permute-start.5
  66.3 8.3 select_maximum_fusion.4
  74.7 25.2 %fusion.37 = f32[1,32,256,128]{3,2,1,0:T(8,128)} fusion(f32[1,32,256,128]{3,2,1,0:T(8,128)} %fusion.52, f32[1,34,258,130]{3,2,1,0:T(8,128)} %select_maximum_fusion.4, f32[1,1,256,128]{3,2,1,0:T(8,128)S(1)} %collective-permute-done.5, f32[1,1,256,128]{3,2,1,0:T(8,128)S(1)} %collective-permute-done.4, f32[1,32,256,128]{3,2,1,0:T(8,128)} %copy-done, ...), kind=kLoop, calls=%fused_computation.66 | loop fusion | flops 36700160 | bytes 46661632 | tf_op jit(solution)/shard_map/add | solution.py:120
  102.8 3.5 collective-permute-start.7
  108.8 8.3 select_maximum_fusion.2
  117.2 25.5 %fusion.22 = f32[1,32,256,128]{3,2,1,0:T(8,128)} fusion(f32[1,32,256,128]{3,2,1,0:T(8,128)} %fusion.37, f32[1,34,258,130]{3,2,1,0:T(8,128)} %select_maximum_fusion.2, f32[1,1,256,128]{3,2,1,0:T(8,128)S(1)} %collective-permute-done.7, f32[1,1,256,128]{3,2,1,0:T(8,128)S(1)} %collective-permute-done.6, f32[1,32,256,128]{3,2,1,0:T(8,128)} %copy-done, ...), kind=kLoop, calls=%fused_computation.45 | loop fusion | flops 36700160 | bytes 46661632 | tf_op jit(solution)/shard_map/add | solution.py:120
  145.5 3.4 collective-permute-start.9
  151.3 8.3 select_maximum_fusion
  159.6 25.2 %fusion.7 = f32[32,256,128]{2,1,0:T(8,128)} fusion(f32[1,32,256,128]{3,2,1,0:T(8,128)} %fusion.22, f32[1,34,258,130]{3,2,1,0:T(8,128)} %select_maximum_fusion, f32[1,1,256,128]{3,2,1,0:T(8,128)S(1)} %collective-permute-done.9, f32[1,1,256,128]{3,2,1,0:T(8,128)S(1)} %collective-permute-done.8, f32[1,32,256,128]{3,2,1,0:T(8,128)} %copy-done, ...), kind=kLoop, calls=%fused_computation.24 | loop fusion | flops 36700160 | bytes 46661632 | tf_op jit(solution)/shard_map/reshape.1
  184.8 6.3 fusion.136
  191.1 3.7 fusion.133
  194.8 4.8 fusion.104
  199.6 4.9 add_bitcast_fusion.2
  204.5 4.5 copy.48
  209.0 9.5 %all-to-all-start = ((f32[1,32,256,128]{3,1,0,2:T(8,128)}), f32[1,32,256,128]{3,1,0,2:T(8,128)}, u32[]{:S(2)}, u32[]{:S(2)}) async-start(f32[1,32,256,128]{3,1,0,2:T(8,128)} %copy.48), calls=%async_computation | async-start | bytes 8388608 | tf_op jit(solution)/shard_map/all_to_all | solution.py:125
  218.5 7.5 fusion.96
  226.0 4.7 subtract_bitcast_fusion.3
  230.8 4.4 copy.52
  235.2 30.7 %all-to-all-done = f32[1,32,256,128]{3,1,0,2:T(8,128)} async-done(((f32[1,32,256,128]{3,1,0,2:T(8,128)}), f32[1,32,256,128]{3,1,0,2:T(8,128)}, u32[]{:S(2)}, u32[]{:S(2)}) %all-to-all-start) | async-done | bytes 4194336 | tf_op jit(solution)/shard_map/all_to_all | solution.py:125
  265.9 5.9 all-to-all-start.2
  271.8 8.2 copy.91
  280.0 39.2 %all-to-all-done.2 = f32[1,32,256,128]{3,1,0,2:T(8,128)} async-done(((f32[1,32,256,128]{3,1,0,2:T(8,128)}), f32[1,32,256,128]{3,1,0,2:T(8,128)}, u32[]{:S(2)}, u32[]{:S(2)}) %all-to-all-start.2) | async-done | bytes 4194336 | tf_op jit(solution)/shard_map/all_to_all | solution.py:132
  319.2 5.6 all-to-all-start.1
  324.8 8.1 copy.90
  333.0 80.9 %all-to-all-done.1 = f32[4,32,64,128]{3,0,1,2:T(4,128)} async-done(((f32[4,32,64,128]{3,0,1,2:T(4,128)}), f32[4,32,64,128]{3,0,1,2:T(4,128)}, u32[]{:S(2)}, u32[]{:S(2)}) %all-to-all-start.1) | async-done | bytes 4194336 | tf_op jit(solution)/shard_map/all_to_all | solution.py:124
  413.8 8.8 all-to-all-start.3
  423.2 2.8 copy.50
  427.9 5.7 fusion.142
  433.7 77.4 %all-to-all-done.3 = f32[4,32,64,128]{3,0,1,2:T(4,128)} async-done(((f32[4,32,64,128]{3,0,1,2:T(4,128)}), f32[4,32,64,128]{3,0,1,2:T(4,128)}, u32[]{:S(2)}, u32[]{:S(2)}) %all-to-all-start.3) | async-done | bytes 4194336 | tf_op jit(solution)/shard_map/all_to_all | solution.py:131
  511.1 2.8 copy.54
  513.9 4.1 fusion.140
  517.9 5.8 add_bitcast_fusion.1
  523.7 5.8 subtract_bitcast_fusion.2
  529.5 5.1 gather_fusion
  534.6 5.0 gather_fusion.1
  539.5 7.5 fusion.78
  547.1 4.1 fusion.144
  551.2 4.1 subtract_bitcast_fusion.1
  555.3 4.5 copy.60
  559.8 9.6 %all-to-all-start.4 = ((f32[4,128,16,128]{3,2,0,1:T(8,128)}), f32[4,128,16,128]{3,2,0,1:T(8,128)}, u32[]{:S(2)}, u32[]{:S(2)}) async-start(f32[4,128,16,128]{3,2,0,1:T(8,128)} %copy.60), calls=%async_computation.4 | async-start | bytes 8388608 | tf_op jit(solution)/shard_map/all_to_all | solution.py:149
  569.4 6.1 fusion.138
  575.5 4.1 add_bitcast_fusion
  579.5 4.4 copy.66
  584.0 74.1 %all-to-all-done.4 = f32[4,128,16,128]{3,2,0,1:T(8,128)} async-done(((f32[4,128,16,128]{3,2,0,1:T(8,128)}), f32[4,128,16,128]{3,2,0,1:T(8,128)}, u32[]{:S(2)}, u32[]{:S(2)}) %all-to-all-start.4) | async-done | bytes 4194336 | tf_op jit(solution)/shard_map/all_to_all | solution.py:149
  658.1 8.9 %all-to-all-start.6 = ((f32[4,128,16,128]{3,2,0,1:T(8,128)}), f32[4,128,16,128]{3,2,0,1:T(8,128)}, u32[]{:S(2)}, u32[]{:S(2)}) async-start(f32[4,128,16,128]{3,2,0,1:T(8,128)} %copy.66), calls=%async_computation.6 | async-start | bytes 8388608 | tf_op jit(solution)/shard_map/all_to_all | solution.py:156
  666.9 4.9 copy.62
  671.8 83.8 %all-to-all-done.6 = f32[4,128,16,128]{3,2,0,1:T(8,128)} async-done(((f32[4,128,16,128]{3,2,0,1:T(8,128)}), f32[4,128,16,128]{3,2,0,1:T(8,128)}, u32[]{:S(2)}, u32[]{:S(2)}) %all-to-all-start.6) | async-done | bytes 4194336 | tf_op jit(solution)/shard_map/all_to_all | solution.py:156
  755.6 7.2 all-to-all-start.5
  762.8 4.8 copy.68
  767.7 42.6 %all-to-all-done.5 = f32[4,32,64,128]{3,2,1,0:T(8,128)} async-done(((f32[4,32,64,128]{3,2,1,0:T(8,128)}), f32[4,32,64,128]{3,2,1,0:T(8,128)}, u32[]{:S(2)}, u32[]{:S(2)}) %all-to-all-start.5) | async-done | bytes 4194336 | tf_op jit(solution)/shard_map/all_to_all | solution.py:148
  810.2 5.7 all-to-all-start.7
  818.4 7.1 fusion.92
  825.6 7.3 fusion.101
  832.9 30.5 %all-to-all-done.7 = f32[4,32,64,128]{3,2,1,0:T(8,128)} async-done(((f32[4,32,64,128]{3,2,1,0:T(8,128)}), f32[4,32,64,128]{3,2,1,0:T(8,128)}, u32[]{:S(2)}, u32[]{:S(2)}) %all-to-all-start.7) | async-done | bytes 4194336 | tf_op jit(solution)/shard_map/all_to_all | solution.py:155
  865.8 4.8 fusion.99
  870.6 4.8 fusion.94
  875.4 3.9 fusion.72
  879.3 5.4 subtract_bitcast_fusion
  (63 shorter events, 29.1 us)
Async XLA Ops:
  1.6 14.3 %copy-start.10 = (f32[1,32,256,128]{3,2,1,0:T(8,128)S(1)}, f32[1,32,256,128]{3,2,1,0:T(8,128)}, u32[]{:S(2)}) copy-start(f32[1,32,256,128]{3,2,1,0:T(8,128)} %param.7) | copy-start | bytes 12582916
  10.6 15.1 %copy-start = (f32[1,32,256,128]{3,2,1,0:T(8,128)}, f32[1,32,256,128]{3,2,1,0:T(8,128)S(1)}, u32[]{:S(2)}) copy-start(f32[1,32,256,128]{3,2,1,0:T(8,128)S(1)} %select_select_fusion) | copy-start | bytes 12582916
  10.7 10.6 %collective-permute-start = (f32[1,1,256,128]{3,2,1,0:T(8,128)S(1)}, f32[1,1,256,128]{3,2,1,0:T(8,128)S(1)}, u32[]{:S(2)}, u32[]{:S(2)}) collective-permute-start(f32[1,1,256,128]{3,2,1,0:T(8,128)S(1)} %get-tuple-element.15), channel_id=1, source_target_pairs={{4,0},{8,4},{12,8},{5,1},{9,5},{13,9},{6,2},{10,6},{14,10},{7,3},{... | collective-permute-start | bytes 393224 | tf_op jit(solution)/shard_map/ppermute | solution.py:25
  12.6 8.7 collective-permute-start.2
  16.0 9.7 %collective-permute-start.1 = (f32[1,1,256,128]{3,2,1,0:T(8,128)S(1)}, f32[1,1,256,128]{3,2,1,0:T(8,128)S(1)}, u32[]{:S(2)}, u32[]{:S(2)}) collective-permute-start(f32[1,1,256,128]{3,2,1,0:T(8,128)S(1)} %get-tuple-element.17), channel_id=1, source_target_pairs={{4,0},{8,4},{12,8},{5,1},{9,5},{13,9},{6,2},{10,6},{14,10},{7,3},{... | collective-permute-start | bytes 393224 | tf_op jit(solution)/shard_map/ppermute | solution.py:25
  17.9 7.8 collective-permute-start.3
  58.4 5.7 collective-permute-start.4
  60.3 6.0 collective-permute-start.5
  100.9 5.7 collective-permute-start.6
  102.8 6.0 collective-permute-start.7
  143.6 5.7 collective-permute-start.8
  145.5 5.7 collective-permute-start.9
  184.8 6.3 copy-start.8
  191.1 3.7 copy-start.9
  194.8 4.8 copy-start.4
  209.0 56.9 %all-to-all-start = ((f32[1,32,256,128]{3,1,0,2:T(8,128)}), f32[1,32,256,128]{3,1,0,2:T(8,128)}, u32[]{:S(2)}, u32[]{:S(2)}) async-start(f32[1,32,256,128]{3,1,0,2:T(8,128)} %copy.48), calls=%async_computation | async-start | bytes 8388608 | tf_op jit(solution)/shard_map/all_to_all | solution.py:125
  218.5 7.5 copy-start.5
  265.9 53.3 %all-to-all-start.2 = ((f32[1,32,256,128]{3,1,0,2:T(8,128)}), f32[1,32,256,128]{3,1,0,2:T(8,128)}, u32[]{:S(2)}, u32[]{:S(2)}) async-start(f32[1,32,256,128]{3,1,0,2:T(8,128)} %copy.52), calls=%async_computation.2 | async-start | bytes 8388608 | tf_op jit(solution)/shard_map/all_to_all | solution.py:132
  319.2 94.7 %all-to-all-start.1 = ((f32[4,32,64,128]{3,0,1,2:T(4,128)}), f32[4,32,64,128]{3,0,1,2:T(4,128)}, u32[]{:S(2)}, u32[]{:S(2)}) async-start(f32[4,32,64,128]{3,0,1,2:T(4,128)} %bitcast.158), calls=%async_computation.1 | async-start | bytes 8388608 | tf_op jit(solution)/shard_map/all_to_all | solution.py:124
  413.8 8.8 copy-start.14
  413.8 8.9 %copy-start.15 = (s32[4]{0:T(128)S(1)}, s32[4]{0:T(128)}, u32[]{:S(2)}) copy-start(s32[4]{0:T(128)} %param.11) | copy-start | bytes 52
  413.8 97.2 %all-to-all-start.3 = ((f32[4,32,64,128]{3,0,1,2:T(4,128)}), f32[4,32,64,128]{3,0,1,2:T(4,128)}, u32[]{:S(2)}, u32[]{:S(2)}) async-start(f32[4,32,64,128]{3,0,1,2:T(4,128)} %bitcast.156), calls=%async_computation.3 | async-start | bytes 8388608 | tf_op jit(solution)/shard_map/all_to_all | solution.py:131
  426.0 2.0 copy-start.6
  513.8 4.1 copy-start.12
  517.9 5.8 copy-start.7
  547.0 4.1 copy-start.1
  547.1 4.1 copy-start.3
  559.8 98.3 %all-to-all-start.4 = ((f32[4,128,16,128]{3,2,0,1:T(8,128)}), f32[4,128,16,128]{3,2,0,1:T(8,128)}, u32[]{:S(2)}, u32[]{:S(2)}) async-start(f32[4,128,16,128]{3,2,0,1:T(8,128)} %copy.60), calls=%async_computation.4 | async-start | bytes 8388608 | tf_op jit(solution)/shard_map/all_to_all | solution.py:149
  569.4 6.1 copy-start.2
  658.1 97.6 %all-to-all-start.6 = ((f32[4,128,16,128]{3,2,0,1:T(8,128)}), f32[4,128,16,128]{3,2,0,1:T(8,128)}, u32[]{:S(2)}, u32[]{:S(2)}) async-start(f32[4,128,16,128]{3,2,0,1:T(8,128)} %copy.66), calls=%async_computation.6 | async-start | bytes 8388608 | tf_op jit(solution)/shard_map/all_to_all | solution.py:156
  755.6 54.6 %all-to-all-start.5 = ((f32[4,32,64,128]{3,2,1,0:T(8,128)}), f32[4,32,64,128]{3,2,1,0:T(8,128)}, u32[]{:S(2)}, u32[]{:S(2)}) async-start(f32[4,32,64,128]{3,2,1,0:T(8,128)} %bitcast.159), calls=%async_computation.5 | async-start | bytes 8388608 | tf_op jit(solution)/shard_map/all_to_all | solution.py:148
  810.2 53.1 %all-to-all-start.7 = ((f32[4,32,64,128]{3,2,1,0:T(8,128)}), f32[4,32,64,128]{3,2,1,0:T(8,128)}, u32[]{:S(2)}, u32[]{:S(2)}) async-start(f32[4,32,64,128]{3,2,1,0:T(8,128)} %bitcast.157), calls=%async_computation.7 | async-start | bytes 8388608 | tf_op jit(solution)/shard_map/all_to_all | solution.py:155
  870.6 4.8 copy-start.11
  875.4 3.9 copy-start.13
where the time goes:
time: 899 us; the launch traced here: 885 us
  waiting for transfers between devices  467 us (52%)
  other arithmetic  154 us (17%)
  matrix products  105 us (12%)
  starting transfers between devices  87.7 us (10%)
  local copies, waits for them, and re-layouts  71.1 us (8%)
    dot_general x20, matrix products, multiply_along(): jnp.einsum(FORMS[axis_dim], values, matrix, precision=lax.Precision.HIGHEST)  105 us
    all_to_all x1, waiting for transfers between devices, local(): lax.all_to_all(cross_imag, 'slab', split_axis=1, concat_axis=2, tiled=True)  83.8 us
    all_to_all x1, waiting for transfers between devices, local(): lax.all_to_all(lax.all_to_all(real_part, 'pair', split_axis=2, concat_axi...  80.9 us
    all_to_all x1, waiting for transfers between devices, local(): lax.all_to_all(lax.all_to_all(imag_part, 'pair', split_axis=2, concat_axi...  77.4 us
    add x3, other arithmetic, local(): volume = volume + STEP_SIZE * change  76 us
    all_to_all x1, waiting for transfers between devices, local(): lax.all_to_all(cross_real, 'slab', split_axis=1, concat_axis=2, tiled=True)  74.1 us
    all_to_all x1, waiting for transfers between devices, local(): lax.all_to_all(lax.all_to_all(cross_real, 'slab', split_axis=1, concat_ax...  42.6 us
    all_to_all x1, waiting for transfers between devices, local(): lax.all_to_all(imag_part, 'pair', split_axis=2, concat_axis=0, tiled=True)  39.2 us
  transfers between devices with their start and end apart: 18, of which 14 were waited for; matrix products, arithmetic and copies ran while one was open for 10% of the time, Pallas kernels for 0%

commit v1 on v0

--- a/solution.py
+++ b/solution.py
@@ -1,16 +1,23 @@
+import functools
 import math
 
 import jax
 import jax.numpy as jnp
+import ml_dtypes
+import numpy as np
 from jax import lax
+from jax.experimental import pallas as pl
+from jax.experimental.pallas import tpu as pltpu
 from jax.sharding import PartitionSpec as P
 
-X = 256
 STEPS = 4
-
-
 STEP_SIZE = 1.0 / 6.0
 FLOOR_VALUE = 0.01
+PAD = 8
+LIMIT = 58 * 1024 * 1024
+MESH = pl.DeviceIdType.MESH
+
+
 FORMS = {1: "bjxy,jk->bkxy", 2: "bzjy,jk->bzky", 3: "bzxj,jk->bzxk"}
 
 
@@ -87,12 +94,12 @@
     return jnp.where(counter < length // 2, counter, counter - length).astype(jnp.float32) / length
 
 
-def cross_power(own_real, own_imag, far_real, far_imag, decay_rate, offset):
+def cross_power(own_real, own_imag, far_real, far_imag, decay_rate, offset, whole_rows):
     depth_count = own_real.shape[1]
     row_count = own_real.shape[2]
     width_count = own_real.shape[3]
     along_depth = signed_frequency(jnp.arange(depth_count, dtype=jnp.int32), depth_count)
-    along_rows = signed_frequency(offset + jnp.arange(row_count, dtype=jnp.int32), X)
+    along_rows = signed_frequency(offset + jnp.arange(row_count, dtype=jnp.int32), whole_rows)
     along_width = signed_frequency(jnp.arange(width_count, dtype=jnp.int32), width_count)
     radius = (
         along_depth[:, None, None] ** 2
@@ -106,7 +113,26 @@
     return (cross_real * weight, cross_imag * weight)
 
 
-def local(occupancy, classes, conductance, damping, matches):
+def picked(values, matches):
+    return jnp.stack(
+        [
+            lax.dynamic_index_in_dim(values, matches[i], 0, keepdims=False)
+            for i in range(matches.shape[0])
+        ]
+    )
+
+
+def spread(values):
+    values = lax.all_to_all(values, "pair", split_axis=2, concat_axis=0, tiled=True)
+    return lax.all_to_all(values, "slab", split_axis=2, concat_axis=1, tiled=True)
+
+
+def gathered(values):
+    values = lax.all_to_all(values, "slab", split_axis=1, concat_axis=2, tiled=True)
+    return lax.all_to_all(values, "pair", split_axis=0, concat_axis=2, tiled=True)
+
+
+def plain(occupancy, classes, conductance, damping, matches):
     conduct = jnp.zeros(occupancy.shape, jnp.float32)
     for class_id in range(conductance.shape[0]):
         conduct = jnp.where(classes == class_id, conductance[class_id], conduct)
@@ -118,50 +144,549 @@
         for other_field, other_conduct in zip(beside_all, outer_rims):
             change = change + 0.5 * (conduct + other_conduct) * (other_field - volume)
         volume = volume + STEP_SIZE * change
+    whole_rows = volume.shape[2]
     real_part, imag_part = forward_real(volume, 3)
     real_part, imag_part = forward_complex(real_part, imag_part, 2)
-    real_part, imag_part = (
-        lax.all_to_all(
-            lax.all_to_all(real_part, "pair", split_axis=2, concat_axis=0, tiled=True),
-            "slab",
-            split_axis=2,
-            concat_axis=1,
-            tiled=True,
-        ),
-        lax.all_to_all(
-            lax.all_to_all(imag_part, "pair", split_axis=2, concat_axis=0, tiled=True),
-            "slab",
-            split_axis=2,
-            concat_axis=1,
-            tiled=True,
-        ),
-    )
+    real_part, imag_part = (spread(real_part), spread(imag_part))
     real_part, imag_part = forward_complex(real_part, imag_part, 1)
-    far_real = jnp.take(real_part, matches, axis=0)
-    far_imag = jnp.take(imag_part, matches, axis=0)
+    far_real = picked(real_part, matches)
+    far_imag = picked(imag_part, matches)
     offset = (
         lax.axis_index("pair") * lax.axis_size("slab") + lax.axis_index("slab")
     ) * real_part.shape[2]
-    cross_real, cross_imag = cross_power(real_part, imag_part, far_real, far_imag, damping, offset)
+    cross_real, cross_imag = cross_power(
+        real_part, imag_part, far_real, far_imag, damping, offset, whole_rows
+    )
     cross_real, cross_imag = inverse_complex(cross_real, cross_imag, 1)
-    back_real, back_imag = (
-        lax.all_to_all(
-            lax.all_to_all(cross_real, "slab", split_axis=1, concat_axis=2, tiled=True),
-            "pair",
-            split_axis=0,
-            concat_axis=2,
-            tiled=True,
-        ),
-        lax.all_to_all(
-            lax.all_to_all(cross_imag, "slab", split_axis=1, concat_axis=2, tiled=True),
-            "pair",
-            split_axis=0,
-            concat_axis=2,
-            tiled=True,
-        ),
-    )
+    back_real, back_imag = (gathered(cross_real), gathered(cross_imag))
     back_real, back_imag = inverse_complex(back_real, back_imag, 2)
     return inverse_real(back_real, back_imag, 3)
+
+
+def halves(matrix):
+    high = matrix.astype(np.float32).astype(ml_dtypes.bfloat16)
+    low = (matrix - high.astype(np.float64)).astype(ml_dtypes.bfloat16)
+    return high, low
+
+
+def trig(rows, cols, length):
+    angle = 2.0 * np.pi * ((np.asarray(rows)[:, None] * np.asarray(cols)[None, :]) % length) / length
+    return np.cos(angle) / math.sqrt(length), np.sin(angle) / math.sqrt(length)
+
+
+def swapped(matrix, axis):
+    first, second = np.split(matrix, 2, axis)
+    return np.concatenate([second, -first], axis)
+
+
+def row_order(length, blocks):
+    half = length // blocks // 2
+    order = []
+    for block in range(blocks):
+        ahead = [block * half + j for j in range(half)]
+        order += ahead + [(length - k) if k else length // 2 for k in ahead]
+    return np.array(order)
+
+
+def forward_y(length):
+    half = length // 2
+    cosine, sine = trig(np.arange(length), np.arange(half), length)
+    imag = -sine
+    imag[:, 0] = (1.0 - 2.0 * (np.arange(length) % 2)) / math.sqrt(length)
+    table = np.concatenate([cosine, imag], 1)
+    return np.concatenate([table, swapped(table, 1)], 1)
+
+
+def inverse_y(length):
+    half = length // 2
+    cosine, sine = trig(np.arange(half), np.arange(length), length)
+    real, imag = 2.0 * cosine, -2.0 * sine
+    real[0] = 1.0 / math.sqrt(length)
+    imag[0] = (1.0 - 2.0 * (np.arange(length) % 2)) / math.sqrt(length)
+    table = np.concatenate([real, imag], 0)
+    other = np.concatenate([-imag, real], 0)
+    return np.concatenate([table, other], 1)
+
+
+def forward_x(length, blocks):
+    cosine, sine = trig(row_order(length, blocks), np.arange(length), length)
+    return np.concatenate([cosine, sine], 1)
+
+
+def inverse_x(length, blocks):
+    cosine, sine = trig(np.arange(length), row_order(length, blocks), length)
+    return np.concatenate([cosine, -sine], 1)
+
+
+def both_z(length):
+    cosine, sine = trig(np.arange(length), np.arange(length), length)
+    return np.concatenate([cosine, sine], 1), np.concatenate([cosine, -sine], 1)
+
+
+def squared(length):
+    counter = np.arange(length)
+    return (np.where(counter < length // 2, counter, counter - length) / length) ** 2
+
+
+def radii(depth, width):
+    half = width // 2
+    lanes = np.arange(width) % half
+    along = squared(width)[lanes]
+    first = squared(depth)[:, None] + along[None, :]
+    other = along.copy()
+    other[lanes == 0] = 0.25
+    second = squared(depth)[:, None] + other[None, :]
+    corner = np.zeros(width)
+    corner[lanes == 1], corner[lanes == 2], corner[lanes == 3] = 0.25, 0.25, 0.5
+    third = squared(depth)[:, None] + corner[None, :]
+    return np.stack([first, second, third]).astype(np.float32)
+
+
+def split(values):
+    high = values.astype(jnp.bfloat16)
+    return high, (values - high.astype(jnp.float32)).astype(jnp.bfloat16)
+
+
+def dot(a, b):
+    return jnp.dot(a, b, preferred_element_type=jnp.float32)
+
+
+def left(matrix, values):
+    high, low = split(values)
+    return dot(matrix[0][...], high) + (dot(matrix[0][...], low) + dot(matrix[1][...], high))
+
+
+def right(values, matrix):
+    high, low = split(values)
+    return dot(high, matrix[0][...]) + (dot(low, matrix[0][...]) + dot(high, matrix[1][...]))
+
+
+def planes_transformed(first, second, along_y, along_x):
+    rows, lanes = first.shape
+    mid = right(jnp.concatenate([first, second], 0), along_y)
+    mid = jnp.concatenate(
+        [
+            jnp.concatenate([mid[:rows, :lanes], mid[rows:, :lanes]], 1),
+            jnp.concatenate([mid[:rows, lanes:], mid[rows:, lanes:]], 1),
+        ],
+        0,
+    )
+    out = left(along_x, mid)
+    return out[:, :lanes], out[:, lanes:]
+
+
+def diffuse_kernel(
+    slabs, cond, occ, cls, yh, yl, xh, xl, out, buf_a, buf_b, cx, cy, cz, kept, halo, ends, send, recv
+):
+    depth, rows, lanes = occ.shape
+    tile = min(64, rows)
+    me = lax.axis_index("slab")
+    has_low, has_high = me > 0, me < slabs - 1
+    low, high = lax.max(me - 1, 0), lax.min(me + 1, slabs - 1)
+
+    barrier = pltpu.get_barrier_semaphore()
+
+    @pl.when(has_low)
+    def _():
+        pl.semaphore_signal(barrier, inc=1, device_id={"slab": low}, device_id_type=MESH)
+
+    @pl.when(has_high)
+    def _():
+        pl.semaphore_signal(barrier, inc=1, device_id={"slab": high}, device_id_type=MESH)
+
+    inside = pl.ds(PAD, rows)
+
+    def conduct(plane):
+        labels = cls[plane]
+        value = jnp.full((rows, lanes), cond[0], jnp.float32)
+        for k in range(1, cond.shape[0]):
+            value = jnp.where(labels == k, cond[k], value)
+        return value
+
+    ends[0] = conduct(0)
+    ends[1] = conduct(depth - 1)
+
+    pl.semaphore_wait(barrier, lax.min(me, 1) + lax.min(slabs - 1 - me, 1))
+
+    def copies(slot, lowest, highest):
+        down = pltpu.make_async_remote_copy(
+            lowest, halo.at[slot, 1], send.at[slot, 0], recv.at[slot, 1],
+            device_id={"slab": low}, device_id_type=MESH,
+        )
+        up = pltpu.make_async_remote_copy(
+            highest, halo.at[slot, 0], send.at[slot, 1], recv.at[slot, 0],
+            device_id={"slab": high}, device_id_type=MESH,
+        )
+        return down, up
+
+    def begin(pair):
+        pl.when(has_low)(lambda: pair[0].start())
+        pl.when(has_high)(lambda: pair[1].start())
+
+    def arrived(pair):
+        pl.when(has_low)(lambda: pair[1].wait_recv())
+        pl.when(has_high)(lambda: pair[0].wait_recv())
+
+    def sent(pair):
+        pl.when(has_low)(lambda: pair[0].wait_send())
+        pl.when(has_high)(lambda: pair[1].wait_send())
+
+    kappas = copies(STEPS, ends.at[0], ends.at[1])
+    begin(kappas)
+    fields = copies(0, occ.at[0], occ.at[depth - 1])
+    begin(fields)
+
+    for slot in range(STEPS + 1):
+
+        @pl.when(jnp.logical_not(has_low))
+        def _():
+            halo[slot, 0] = jnp.zeros((rows, lanes), jnp.float32)
+
+        @pl.when(jnp.logical_not(has_high))
+        def _():
+            halo[slot, 1] = jnp.zeros((rows, lanes), jnp.float32)
+
+    edge = jnp.zeros((PAD, lanes), jnp.float32)
+
+    @pl.loop(0, depth)
+    def _(z):
+        buf_b[z, inside] = conduct(z)
+        buf_a[z, inside] = occ[z]
+        for ref in (buf_a, buf_b):
+            ref[z, pl.ds(0, PAD)] = edge
+            ref[z, pl.ds(PAD + rows, PAD)] = edge
+
+    scale = 0.5 * STEP_SIZE
+
+    @pl.loop(0, depth)
+    def _(z):
+        cx[z, pl.ds(0, PAD)] = scale * (buf_b[z, pl.ds(0, PAD)] + buf_b[z, pl.ds(1, PAD)])
+        for r in range(0, rows, tile):
+            here = buf_b[z, pl.ds(PAD + r, tile)]
+            x_next = buf_b[z, pl.ds(PAD + r + 1, tile)]
+            cx[z, pl.ds(PAD + r, tile)] = scale * (here + x_next)
+            lane = lax.broadcasted_iota(jnp.int32, (tile, lanes), 1)
+            y_next = pltpu.roll(here, lanes - 1, 1)
+            cy[z, pl.ds(r, tile)] = jnp.where(lane == lanes - 1, 0.0, scale * (here + y_next))
+            rim = (lane == 0) | (lane == lanes - 1)
+            kept[z, pl.ds(r, tile)] = 1.0 - jnp.where(rim, scale * here, 0.0)
+
+    @pl.loop(0, depth - 1)
+    def _(z):
+        cz[z + 1] = scale * (buf_b[z, inside] + buf_b[z + 1, inside])
+
+    arrived(kappas)
+    cz[0] = scale * (buf_b[0, inside] + halo[STEPS, 0])
+    cz[depth] = scale * (buf_b[depth - 1, inside] + halo[STEPS, 1])
+
+    def update(src, dst, z, r, here, flux_low, flux_high):
+        x_next = src[z, pl.ds(PAD + r + 1, tile)]
+        x_last = src[z, pl.ds(PAD + r - 1, tile)]
+        along_x = cx[z, pl.ds(PAD + r, tile)] * (x_next - here) - cx[
+            z, pl.ds(PAD + r - 1, tile)
+        ] * (here - x_last)
+        flux = cy[z, pl.ds(r, tile)] * (pltpu.roll(here, lanes - 1, 1) - here)
+        along_y = flux - pltpu.roll(flux, 1, 1)
+        dst[z, pl.ds(PAD + r, tile)] = kept[z, pl.ds(r, tile)] * here + (
+            along_x + along_y + (flux_high - flux_low)
+        )
+
+    bufs = (buf_a, buf_b)
+    for step in range(STEPS):
+        src, dst = bufs[step % 2], bufs[1 - step % 2]
+        arrived(fields)
+        sent(fields)
+        for r in range(0, rows, tile):
+            at, within = pl.ds(PAD + r, tile), pl.ds(r, tile)
+            here, after = src[0, at], src[1, at]
+            update(
+                src, dst, 0, r, here,
+                cz[0, within] * (here - halo[step, 0, within]),
+                cz[1, within] * (after - here),
+            )
+            here, before = src[depth - 1, at], src[depth - 2, at]
+            update(
+                src, dst, depth - 1, r, here,
+                cz[depth - 1, within] * (here - before),
+                cz[depth, within] * (halo[step, 1, within] - here),
+            )
+        if step + 1 < STEPS:
+            fields = copies(
+                step + 1, dst.at[0, inside], dst.at[depth - 1, inside]
+            )
+            begin(fields)
+        for r in range(0, rows, tile):
+            at, within = pl.ds(PAD + r, tile), pl.ds(r, tile)
+
+            def body(z, carry):
+                here, flux_low = carry
+                after = src[z + 1, at]
+                flux_high = cz[z + 1, within] * (after - here)
+                update(src, dst, z, r, here, flux_low, flux_high)
+                return after, flux_high
+
+            first = src[1, at]
+            lax.fori_loop(1, depth - 1, body, (first, cz[1, within] * (first - src[0, at])))
+    sent(kappas)
+
+    field = bufs[STEPS % 2]
+
+    @pl.loop(0, depth // 2)
+    def _(i):
+        one, two = planes_transformed(
+            field[2 * i, inside], field[2 * i + 1, inside], (yh, yl), (xh, xl)
+        )
+        out[2 * i] = one
+        out[2 * i + 1] = two
+
+
+def diffused(occupancy, classes, conductance, slabs, pairs):
+    depth, rows, lanes = occupancy.shape
+    vmem = pl.BlockSpec(memory_space=pltpu.VMEM)
+    y = halves(forward_y(lanes))
+    x = halves(forward_x(rows, slabs * pairs))
+    padded = (depth, rows + 2 * PAD, lanes)
+    return pl.pallas_call(
+        functools.partial(diffuse_kernel, slabs),
+        out_shape=jax.ShapeDtypeStruct((depth, rows, lanes), jnp.float32),
+        in_specs=[pl.BlockSpec(memory_space=pltpu.SMEM)] + [vmem] * 6,
+        out_specs=vmem,
+        scratch_shapes=[
+            pltpu.VMEM(padded, jnp.float32),
+            pltpu.VMEM(padded, jnp.float32),
+            pltpu.VMEM((depth, rows + PAD, lanes), jnp.float32),
+            pltpu.VMEM((depth, rows, lanes), jnp.float32),
+            pltpu.VMEM((depth + 1, rows, lanes), jnp.float32),
+            pltpu.VMEM((depth, rows, lanes), jnp.float32),
+            pltpu.VMEM((STEPS + 1, 2, rows, lanes), jnp.float32),
+            pltpu.VMEM((2, rows, lanes), jnp.float32),
+            pltpu.SemaphoreType.DMA((STEPS + 1, 2)),
+            pltpu.SemaphoreType.DMA((STEPS + 1, 2)),
+        ],
+        compiler_params=pltpu.CompilerParams(
+            collective_id=0, has_side_effects=True, vmem_limit_bytes=LIMIT
+        ),
+        name="diffuse",
+    )(conductance, occupancy, classes, *y, *x)
+
+
+def exchange_kernel(slabs, pairs, pick, src, dst, own_sem, send, recv):
+    slab, pair = lax.axis_index("slab"), lax.axis_index("pair")
+    shifts = [
+        (dp, dq)
+        for dq in sorted(range(slabs), key=lambda q: -min(q, slabs - q))
+        for dp in range(pairs)
+        if (dp, dq) != (0, 0)
+    ]
+    barrier = pltpu.get_barrier_semaphore()
+    peers = [(lax.rem(pair + dp, pairs), lax.rem(slab + dq, slabs)) for dp, dq in shifts]
+    for p, q in peers:
+        pl.semaphore_signal(barrier, inc=1, device_id={"pair": p, "slab": q}, device_id_type=MESH)
+    pl.semaphore_wait(barrier, len(peers))
+    copies = []
+    for i, (p, q) in enumerate(peers):
+        source, target = pick(src, dst, pair, slab, p, q)
+        copy = pltpu.make_async_remote_copy(
+            source, target, send.at[i], recv.at[i],
+            device_id={"pair": p, "slab": q}, device_id_type=MESH,
+        )
+        copy.start()
+        copies.append(copy)
+    source, target = pick(src, dst, pair, slab, pair, slab)
+    own = pltpu.make_async_copy(source, target, own_sem)
+    own.start()
+    own.wait()
+    for copy in copies:
+        copy.wait_recv()
+    for copy in copies:
+        copy.wait_send()
+
+
+def exchange(values, shape, pick, slabs, pairs, collective_id, name):
+    anywhere = pl.BlockSpec(memory_space=pl.ANY)
+    count = slabs * pairs - 1
+    return pl.pallas_call(
+        functools.partial(exchange_kernel, slabs, pairs, pick),
+        out_shape=jax.ShapeDtypeStruct(shape, jnp.float32),
+        in_specs=[anywhere],
+        out_specs=anywhere,
+        scratch_shapes=[
+            pltpu.SemaphoreType.DMA,
+            pltpu.SemaphoreType.DMA((count,)),
+            pltpu.SemaphoreType.DMA((count,)),
+        ],
+        compiler_params=pltpu.CompilerParams(collective_id=collective_id, has_side_effects=True),
+        name=name,
+    )(values)
+
+
+def half_turn(values):
+    return pltpu.roll(values, values.shape[1] // 2, 1)
+
+
+def cross_kernel(rows, total, place, matches, damping, radius, fh, fl, ih, il, src, out, spec, mags):
+    maps, depth = len(matches.shape) and matches.shape[0], radius.shape[1]
+    lanes = radius.shape[2]
+    half = rows // 2
+    lane = lax.broadcasted_iota(jnp.int32, (depth, lanes), 1)
+    left_half = lane < lanes // 2
+    real0, imag0 = lane == 0, lane == lanes // 2
+    packed = real0 | imag0
+    sign = jnp.where(left_half, 1.0, -1.0)
+    first_device = place[0] == 0
+
+    def load(s, r):
+        return src[s, pl.ds(r, depth, stride=rows)]
+
+    def turned(values):
+        return half_turn(values) * sign
+
+    def along_z(matrix, items):
+        stacked = [jnp.concatenate([v, turned(v)], 0) for v in items]
+        result = left(matrix, jnp.concatenate(stacked, 1))
+        return [result[:, i * lanes : (i + 1) * lanes] for i in range(len(items))]
+
+    def crossed(s, row, fx2):
+        own = spec[row, s]
+        far = spec[row, matches[s]]
+        straight = own * far
+        skew = own * half_turn(far)
+        value = jnp.where(left_half, straight, skew) + half_turn(
+            jnp.where(left_half, -skew, straight)
+        )
+        power = mags[row, s] * mags[row, matches[s]] + FLOOR_VALUE**2
+        return value * (jnp.exp(-damping[s] * (radius[row] + fx2)) * lax.rsqrt(power))
+
+    def keep(row, s, value):
+        spec[row, s] = value
+        square = value * value
+        mags[row, s] = square + half_turn(square)
+
+    def pair_of_rows(j, special):
+        k = place[0] * half + j
+        fx = k.astype(jnp.float32) / total if not isinstance(k, int) else k / total
+        fx2 = fx * fx
+        count = 3 if special else 2
+        items = []
+        for s in range(maps):
+            a, b = load(s, j), load(s, j + half)
+            total_ab, diff = a + b, a - b
+            mixed_a = 0.5 * jnp.where(real0, total_ab, diff)
+            mixed_b = 0.5 * half_turn(jnp.where(imag0, total_ab, -diff))
+            items += [jnp.where(packed, mixed_a, a), jnp.where(packed, mixed_b, b)]
+            if special:
+                corner = jnp.where(real0, a, 0.0)
+                corner = jnp.where(lane == 1, pltpu.roll(a, 1 + lanes // 2, 1), corner)
+                corner = jnp.where(lane == 2, pltpu.roll(b, 2, 1), corner)
+                corner = jnp.where(lane == 3, pltpu.roll(b, 3 + lanes // 2, 1), corner)
+                items.append(corner)
+        for i, value in enumerate(along_z((fh, fl), items)):
+            keep(i % count, i // count, value)
+        second = jnp.where(first_device, 0.25, fx2) if special else fx2
+        items = []
+        for s in range(maps):
+            items += [crossed(s, 0, fx2), crossed(s, 1, second)]
+            if special:
+                items.append(crossed(s, 2, 0.0))
+        items = along_z((ih, il), items)
+        for s in range(maps):
+            a, b = items[s * count], items[s * count + 1]
+            t = half_turn(b)
+            mixed_a = jnp.where(real0, a - t, a + t)
+            mixed_b = jnp.where(real0, a + t, t - a)
+            if special:
+                e = items[s * count + 2]
+                corner_a = jnp.where(real0, e, pltpu.roll(e, lanes // 2 - 1, 1))
+                corner_b = jnp.where(
+                    real0, pltpu.roll(e, lanes - 2, 1), pltpu.roll(e, lanes // 2 - 3, 1)
+                )
+                mixed_a = jnp.where(first_device, corner_a, mixed_a)
+                mixed_b = jnp.where(first_device, corner_b, mixed_b)
+            out[s, pl.ds(j, depth, stride=rows)] = jnp.where(packed, mixed_a, a)
+            out[s, pl.ds(j + half, depth, stride=rows)] = jnp.where(packed, mixed_b, b)
+
+    pair_of_rows(0, True)
+
+    @pl.loop(1, half)
+    def _(j):
+        pair_of_rows(j, False)
+
+
+def crossed_back(values, damping, matches, place, total):
+    maps, depth, rows, lanes = values.shape
+    vmem, smem = pl.BlockSpec(memory_space=pltpu.VMEM), pl.BlockSpec(memory_space=pltpu.SMEM)
+    forward, backward = both_z(depth)
+    result = pl.pallas_call(
+        functools.partial(cross_kernel, rows, total),
+        out_shape=jax.ShapeDtypeStruct((maps, depth * rows, lanes), jnp.float32),
+        in_specs=[smem] * 3 + [vmem] * 6,
+        out_specs=vmem,
+        scratch_shapes=[
+            pltpu.VMEM((3, maps, depth, lanes), jnp.float32),
+            pltpu.VMEM((3, maps, depth, lanes), jnp.float32),
+        ],
+        compiler_params=pltpu.CompilerParams(vmem_limit_bytes=LIMIT),
+        name="cross",
+    )(
+        place, matches, damping, radii(depth, lanes), *halves(forward), *halves(backward),
+        values.reshape(maps, depth * rows, lanes),
+    )
+    return result.reshape(maps, depth, rows, lanes)
+
+
+def finish_kernel(yh, yl, xh, xl, src, out):
+    blocks, depth, rows, lanes = src.shape
+    for i in range(0, depth, 2):
+        first = src[:, i].reshape(blocks * rows, lanes)
+        second = src[:, i + 1].reshape(blocks * rows, lanes)
+        one, two = planes_transformed(first, second, (yh, yl), (xh, xl))
+        out[i] = one
+        out[i + 1] = two
+
+
+def finished(values):
+    blocks, depth, rows, lanes = values.shape
+    step = 4
+    y = halves(inverse_y(lanes))
+    x = halves(inverse_x(blocks * rows, blocks))
+    whole = [pl.BlockSpec(m.shape, lambda i: (0, 0)) for m in (*y, *x)]
+    return pl.pallas_call(
+        finish_kernel,
+        grid=(depth // step,),
+        out_shape=jax.ShapeDtypeStruct((depth, blocks * rows, lanes), jnp.float32),
+        in_specs=whole + [pl.BlockSpec((blocks, step, rows, lanes), lambda i: (0, i, 0, 0))],
+        out_specs=pl.BlockSpec((step, blocks * rows, lanes), lambda i: (i, 0, 0)),
+        compiler_params=pltpu.CompilerParams(vmem_limit_bytes=LIMIT),
+        name="finish",
+    )(*y, *x, values)
+
+
+def fused(slabs, pairs, occupancy, classes, conductance, damping, matches):
+    _, depth, rows, lanes = occupancy.shape
+    maps = damping.shape[0]
+    share = rows // (slabs * pairs)
+    volume = diffused(occupancy[0], classes[0], conductance, slabs, pairs)
+
+    def outward(src, dst, pair, slab, p, q):
+        at = pl.multiple_of((p * slabs + q) * share, share)
+        return (
+            src.at[:, pl.ds(at, share)],
+            dst.at[pair, pl.ds(slab * depth, depth)],
+        )
+
+    columns = exchange(
+        volume, (maps, depth * slabs, share, lanes), outward, slabs, pairs, 1, "spread"
+    )
+    place = (lax.axis_index("pair") * slabs + lax.axis_index("slab")).astype(jnp.int32)
+    columns = crossed_back(columns, damping, matches, place.reshape(1), rows)
+
+    def inward(src, dst, pair, slab, p, q):
+        return src.at[p, pl.ds(q * depth, depth)], dst.at[pair * slabs + slab]
+
+    planes = exchange(
+        columns, (slabs * pairs, depth, share, lanes), inward, slabs, pairs, 2, "gather"
+    )
+    return finished(planes)[None]
 
 
 def solution(mesh):
@@ -173,4 +698,14 @@
         P("groups"),
     )
     out_specs = P(("groups", "pair"), "slab", None, None)
+    slabs, pairs = mesh.shape["slab"], mesh.shape["pair"]
+
+    def local(occupancy, classes, conductance, damping, matches):
+        maps, depth, rows, lanes = occupancy.shape
+        share, rest = divmod(rows, slabs * pairs)
+        fits = rest == 0 and share % 16 == 0 and depth % 8 == 0 and lanes == 128
+        if fits and maps == 1 and damping.shape[0] == pairs:
+            return fused(slabs, pairs, occupancy, classes, conductance, damping, matches)
+        return plain(occupancy, classes, conductance, damping, matches)
+
     return jax.shard_map(local, mesh=mesh, in_specs=in_specs, out_specs=out_specs, check_vma=False)

time: 899 us -> 329 us (0.37); the launches traced: 885 us -> 329 us
  waiting for transfers between devices: 467 us -> 0 us
  Pallas kernels: 0 us -> 329 us
  other arithmetic: 154 us -> 0 us
  matrix products: 105 us -> 0 us
  starting transfers between devices: 87.7 us -> 0 us
  local copies, waits for them, and re-layouts: 71.1 us -> 0 us
    all_to_all x8 -> x0, waiting for transfers between devices: 459 us -> none  [the longest x1 83.8 us: local(): lax.all_to_all(cross_imag, 'slab', split_axis=1, concat_axis=2, tiled=True)]
    pallas_call x0 -> x5, Pallas kernels: none -> 329 us  [the longest x2 189 us: exchange(): pl.pallas_call(functools.partial(exchange_kernel, slabs, pairs, pick), ou...]
    dot_general x20 -> x0, matrix products: 105 us -> none  [multiply_along(): jnp.einsum(FORMS[axis_dim], values, matrix, precision=lax.Precision.HIGHEST)]
    add x5 -> x0, other arithmetic: 76.5 us -> none  [the longest x3 76 us: local(): volume = volume + STEP_SIZE * change]
    all_to_all x8 -> x0, starting transfers between devices: 61.1 us -> none  [the longest x1 9.55 us: local(): lax.all_to_all(cross_real, 'slab', split_axis=1, concat_axis=2, tiled=True)]
    all_to_all x8 -> x0, local copies, waits for them, and re-layouts: 36.6 us -> none  [the longest x1 8.18 us: local(): lax.all_to_all(real_part, 'pair', split_axis=2, concat_axis=0, tiled=True)]
    concatenate x5 -> x0, other arithmetic: 35.7 us -> none  [with_halo(): shard = jnp.concatenate([before, shard, after], axis=dim)]
    ppermute x10 -> x0, starting transfers between devices: 26.6 us -> none  [the longest x5 17 us: with_halo(): before = lax.ppermute(last, axis, up)]
  transfers between devices with their start and end apart: 18 -> 0, of which waited for: 14 -> 0; matrix products, arithmetic and copies ran while one was open for 10% -> 0% of each run, Pallas kernels for 0% -> 0%
where the time goes in v1:
time: 329 us
  Pallas kernels  329 us (100%)
    pallas_call x2, Pallas kernels, exchange(): pl.pallas_call(functools.partial(exchange_kernel, slabs, pairs, pick), ou...  189 us
    pallas_call x1, Pallas kernels, diffused(): pl.pallas_call(functools.partial(diffuse_kernel, slabs), out_shape=jax.Sh...  105 us
    pallas_call x1, Pallas kernels, crossed_back(): pl.pallas_call(functools.partial(cross_kernel, rows, total), out_shape=ja...  20 us
    pallas_call x1, Pallas kernels, finished(): pl.pallas_call(finish_kernel, grid=(depth // step,), out_shape=jax.ShapeD...  13.9 us

profile of v1, /device:TPU:9, one launch (start us, length us, event | category | flops | bytes accessed | tf_op | source)
XLA Modules:
  0.0 328.6 jit_solution(10332531789421954475)
XLA Ops:
  0.0 105.3 %diffuse.1.src = f32[32,256,128]{2,1,0:T(8,128)} custom-call(f32[8]{0:T(128)} %cond.1, f32[32,256,128]{2,1,0:T(8,128)} %bitcast.8, s32[32,256,128]{2,1,0:T(8,128)} %bitcast.9, bf16[128,256]{1,0:T(8,128)(2,1)} %constant.35.clone.yh, bf16[128,256]{1,0:T(8,128)(2,1)} %constant.36.clone.yl, bf16[256,512]{1,0:T(8,128)(2,1)} %constant.37.clone.xh, ...), custom_call_target="tpu_custom_call" | custom-call | tf_op jit(solution)/shard_map/diffuse/pallas_call | solution.py:449
  105.3 95.4 %spread.1 = f32[4,128,16,128]{3,2,1,0:T(8,128)} custom-call(f32[32,256,128]{2,1,0:T(8,128)} %diffuse.1.src), custom_call_target="tpu_custom_call" | custom-call | tf_op jit(solution)/shard_map/spread/pallas_call | solution.py:508
  200.7 20.0 %cross.1 = f32[4,2048,128]{2,1,0:T(8,128)} custom-call(s32[1]{0:T(128)} %bitcast.place, s32[4]{0:T(128)} %matches.1, f32[4]{0:T(128)} %damping.1, f32[3,128,128]{2,1,0:T(8,128)} %constant.39.clone.radius, bf16[128,256]{1,0:T(8,128)(2,1)} %constant.40.clone.fh, bf16[128,256]{1,0:T(8,128)(2,1)} %constant.41.clone.fl, bf16[128,256]{1,0:T(8,128)(2,1)} %constant.42.clone.ih, ...), custom_call_target="tpu_custom_call" | custom-call | tf_op jit(solution)/shard_map/cross/pallas_call | solution.py:619
  220.7 94.0 %gather.1.src = f32[16,32,16,128]{3,2,1,0:T(8,128)} custom-call(f32[4,128,16,128]{3,2,1,0:T(8,128)} %bitcast.7), custom_call_target="tpu_custom_call" | custom-call | tf_op jit(solution)/shard_map/gather/pallas_call | solution.py:508
  314.7 13.9 %finish.1 = f32[32,256,128]{2,1,0:T(8,128)} custom-call(bf16[128,256]{1,0:T(8,128)(2,1)} %constant.44.clone.yh, bf16[128,256]{1,0:T(8,128)(2,1)} %constant.45.clone.yl, bf16[256,512]{1,0:T(8,128)(2,1)} %constant.46.clone.xh, bf16[256,512]{1,0:T(8,128)(2,1)} %constant.47.clone.xl, f32[16,32,16,128]{3,2,1,0:T(8,128)} %gather.1.src), custom_call_target="tpu_custom_call" | custom-call | tf_op jit(solution)/shard_map/finish/pallas_call | solution.py:653

commit v2 on v1

--- a/solution.py
+++ b/solution.py
@@ -276,10 +276,11 @@
 
 
 def diffuse_kernel(
-    slabs, cond, occ, cls, yh, yl, xh, xl, out, buf_a, buf_b, cx, cy, cz, kept, halo, ends, send, recv
+    slabs, cond, occ, cls, yh, yl, xh, xl, out, buf_a, buf_b, cx, cy, cy_last, cz, kept, halo, ends, send, recv
 ):
     depth, rows, lanes = occ.shape
     tile = min(64, rows)
+    group = max(g for g in range(1, 6) if (depth - 2) % g == 0)
     me = lax.axis_index("slab")
     has_low, has_high = me > 0, me < slabs - 1
     low, high = lax.max(me - 1, 0), lax.min(me + 1, slabs - 1)
@@ -368,6 +369,8 @@
             lane = lax.broadcasted_iota(jnp.int32, (tile, lanes), 1)
             y_next = pltpu.roll(here, lanes - 1, 1)
             cy[z, pl.ds(r, tile)] = jnp.where(lane == lanes - 1, 0.0, scale * (here + y_next))
+            y_last = pltpu.roll(here, 1, 1)
+            cy_last[z, pl.ds(r, tile)] = jnp.where(lane == 0, 0.0, scale * (here + y_last))
             rim = (lane == 0) | (lane == lanes - 1)
             kept[z, pl.ds(r, tile)] = 1.0 - jnp.where(rim, scale * here, 0.0)
 
@@ -385,8 +388,9 @@
         along_x = cx[z, pl.ds(PAD + r, tile)] * (x_next - here) - cx[
             z, pl.ds(PAD + r - 1, tile)
         ] * (here - x_last)
-        flux = cy[z, pl.ds(r, tile)] * (pltpu.roll(here, lanes - 1, 1) - here)
-        along_y = flux - pltpu.roll(flux, 1, 1)
+        along_y = cy[z, pl.ds(r, tile)] * (pltpu.roll(here, lanes - 1, 1) - here) - cy_last[
+            z, pl.ds(r, tile)
+        ] * (here - pltpu.roll(here, 1, 1))
         dst[z, pl.ds(PAD + r, tile)] = kept[z, pl.ds(r, tile)] * here + (
             along_x + along_y + (flux_high - flux_low)
         )
@@ -418,15 +422,17 @@
         for r in range(0, rows, tile):
             at, within = pl.ds(PAD + r, tile), pl.ds(r, tile)
 
-            def body(z, carry):
+            def body(i, carry):
                 here, flux_low = carry
-                after = src[z + 1, at]
-                flux_high = cz[z + 1, within] * (after - here)
-                update(src, dst, z, r, here, flux_low, flux_high)
-                return after, flux_high
+                for z in [1 + i * group + g for g in range(group)]:
+                    after = src[z + 1, at]
+                    flux_high = cz[z + 1, within] * (after - here)
+                    update(src, dst, z, r, here, flux_low, flux_high)
+                    here, flux_low = after, flux_high
+                return here, flux_low
 
             first = src[1, at]
-            lax.fori_loop(1, depth - 1, body, (first, cz[1, within] * (first - src[0, at])))
+            lax.fori_loop(0, (depth - 2) // group, body, (first, cz[1, within] * (first - src[0, at])))
     sent(kappas)
 
     field = bufs[STEPS % 2]
@@ -455,6 +461,7 @@
             pltpu.VMEM(padded, jnp.float32),
             pltpu.VMEM(padded, jnp.float32),
             pltpu.VMEM((depth, rows + PAD, lanes), jnp.float32),
+            pltpu.VMEM((depth, rows, lanes), jnp.float32),
             pltpu.VMEM((depth, rows, lanes), jnp.float32),
             pltpu.VMEM((depth + 1, rows, lanes), jnp.float32),
             pltpu.VMEM((depth, rows, lanes), jnp.float32),
@@ -635,27 +642,24 @@
 
 
 def finish_kernel(yh, yl, xh, xl, src, out):
-    blocks, depth, rows, lanes = src.shape
-    for i in range(0, depth, 2):
-        first = src[:, i].reshape(blocks * rows, lanes)
-        second = src[:, i + 1].reshape(blocks * rows, lanes)
-        one, two = planes_transformed(first, second, (yh, yl), (xh, xl))
+    for i in range(0, src.shape[0], 2):
+        one, two = planes_transformed(src[i], src[i + 1], (yh, yl), (xh, xl))
         out[i] = one
         out[i + 1] = two
 
 
-def finished(values):
-    blocks, depth, rows, lanes = values.shape
+def finished(values, blocks):
+    depth, rows, lanes = values.shape
     step = 4
     y = halves(inverse_y(lanes))
-    x = halves(inverse_x(blocks * rows, blocks))
+    x = halves(inverse_x(rows, blocks))
     whole = [pl.BlockSpec(m.shape, lambda i: (0, 0)) for m in (*y, *x)]
     return pl.pallas_call(
         finish_kernel,
         grid=(depth // step,),
-        out_shape=jax.ShapeDtypeStruct((depth, blocks * rows, lanes), jnp.float32),
-        in_specs=whole + [pl.BlockSpec((blocks, step, rows, lanes), lambda i: (0, i, 0, 0))],
-        out_specs=pl.BlockSpec((step, blocks * rows, lanes), lambda i: (i, 0, 0)),
+        out_shape=jax.ShapeDtypeStruct((depth, rows, lanes), jnp.float32),
+        in_specs=whole + [pl.BlockSpec((step, rows, lanes), lambda i: (i, 0, 0))],
+        out_specs=pl.BlockSpec((step, rows, lanes), lambda i: (i, 0, 0)),
         compiler_params=pltpu.CompilerParams(vmem_limit_bytes=LIMIT),
         name="finish",
     )(*y, *x, values)
@@ -681,12 +685,14 @@
     columns = crossed_back(columns, damping, matches, place.reshape(1), rows)
 
     def inward(src, dst, pair, slab, p, q):
-        return src.at[p, pl.ds(q * depth, depth)], dst.at[pair * slabs + slab]
+        return src.at[p, pl.ds(q * depth, depth)], dst.at[
+            :, pl.ds(pl.multiple_of((pair * slabs + slab) * share, share), share)
+        ]
 
     planes = exchange(
-        columns, (slabs * pairs, depth, share, lanes), inward, slabs, pairs, 2, "gather"
-    )
-    return finished(planes)[None]
+        columns, (depth, rows, lanes), inward, slabs, pairs, 2, "gather"
+    )
+    return finished(planes, slabs * pairs)[None]
 
 
 def solution(mesh):

time: 329 us -> 275 us (0.84)
  Pallas kernels: 329 us -> 274 us
    pallas_call x1, Pallas kernels: 105 us -> 51.4 us  [diffused(): pl.pallas_call(functools.partial(diffuse_kernel, slabs), out_shape=jax.Sh...]
where the time goes in v2:
time: 275 us; the launch traced here: 274 us
  Pallas kernels  274 us (100%)
    pallas_call x2, Pallas kernels, exchange(): pl.pallas_call(functools.partial(exchange_kernel, slabs, pairs, pick), ou...  189 us
    pallas_call x1, Pallas kernels, diffused(): pl.pallas_call(functools.partial(diffuse_kernel, slabs), out_shape=jax.Sh...  51.4 us
    pallas_call x1, Pallas kernels, crossed_back(): pl.pallas_call(functools.partial(cross_kernel, rows, total), out_shape=ja...  20 us
    pallas_call x1, Pallas kernels, finished(): pl.pallas_call(finish_kernel, grid=(depth // step,), out_shape=jax.ShapeD...  13.9 us

profile of v2, /device:TPU:9, one launch (start us, length us, event | category | flops | bytes accessed | tf_op | source)
XLA Modules:
  0.0 274.5 jit_solution(12092415244060832069)
XLA Ops:
  0.0 51.4 %diffuse.1.src = f32[32,256,128]{2,1,0:T(8,128)} custom-call(f32[8]{0:T(128)} %cond.1, f32[32,256,128]{2,1,0:T(8,128)} %bitcast.8, s32[32,256,128]{2,1,0:T(8,128)} %bitcast.9, bf16[128,256]{1,0:T(8,128)(2,1)} %constant.35.clone.yh, bf16[128,256]{1,0:T(8,128)(2,1)} %constant.36.clone.yl, bf16[256,512]{1,0:T(8,128)(2,1)} %constant.37.clone.xh, ...), custom_call_target="tpu_custom_call" | custom-call | tf_op jit(solution)/shard_map/diffuse/pallas_call | solution.py:455
  51.4 95.2 %spread.1 = f32[4,128,16,128]{3,2,1,0:T(8,128)} custom-call(f32[32,256,128]{2,1,0:T(8,128)} %diffuse.1.src), custom_call_target="tpu_custom_call" | custom-call | tf_op jit(solution)/shard_map/spread/pallas_call | solution.py:515
  146.6 20.0 %cross.1 = f32[4,2048,128]{2,1,0:T(8,128)} custom-call(s32[1]{0:T(128)} %bitcast.place, s32[4]{0:T(128)} %matches.1, f32[4]{0:T(128)} %damping.1, f32[3,128,128]{2,1,0:T(8,128)} %constant.39.clone.radius, bf16[128,256]{1,0:T(8,128)(2,1)} %constant.40.clone.fh, bf16[128,256]{1,0:T(8,128)(2,1)} %constant.41.clone.fl, bf16[128,256]{1,0:T(8,128)(2,1)} %constant.42.clone.ih, ...), custom_call_target="tpu_custom_call" | custom-call | tf_op jit(solution)/shard_map/cross/pallas_call | solution.py:626
  166.6 94.0 %gather.1.src = f32[32,256,128]{2,1,0:T(8,128)} custom-call(f32[4,128,16,128]{3,2,1,0:T(8,128)} %bitcast.7), custom_call_target="tpu_custom_call" | custom-call | tf_op jit(solution)/shard_map/gather/pallas_call | solution.py:515
  260.5 13.9 %finish.1 = f32[32,256,128]{2,1,0:T(8,128)} custom-call(bf16[128,256]{1,0:T(8,128)(2,1)} %constant.44.clone.yh, bf16[128,256]{1,0:T(8,128)(2,1)} %constant.45.clone.yl, bf16[256,512]{1,0:T(8,128)(2,1)} %constant.46.clone.xh, bf16[256,512]{1,0:T(8,128)(2,1)} %constant.47.clone.xl, f32[32,256,128]{2,1,0:T(8,128)} %gather.1.src), custom_call_target="tpu_custom_call" | custom-call | tf_op jit(solution)/shard_map/finish/pallas_call | solution.py:657
